TPU v7x, 128 devices: a whole 4x4x4 slice. The times are simulated.
128 devices in a mesh: ulysses: 8 (over z, core), ctx: 16 (over x, y).
Axes of the slice: x: 4, y: 4, z: 4, core: 2. Of those that a mesh axis runs over, the one named last changes fastest.
Arguments:
- queries: bfloat16 [8192, 4096], P(('ulysses', 'ctx')), may hold values from -160 to 160
- keys: bfloat16 [8192, 1024], P(('ulysses', 'ctx')), may hold values from -6 to 6
- values: bfloat16 [8192, 1024], P(('ulysses', 'ctx')), may hold values from -6 to 6
- attn_out: bfloat16 [8192, 4096], P(('ulysses', 'ctx')), may hold values from -4 to 4
- out_grad: bfloat16 [8192, 4096], P(('ulysses', 'ctx')), may hold values from -6 to 6
- segment: int32 [8192], replicated, may hold values from 0 to 2, as said below
- span_order: int32 [32], replicated, may hold values from 0 to 31, as said below
Outputs:
- query_grad: bfloat16 [8192, 4096], P(('ulysses', 'ctx'))
- key_grad: bfloat16 [8192, 1024], P(('ulysses', 'ctx'))
- value_grad: bfloat16 [8192, 1024], P(('ulysses', 'ctx'))
Inputs may be any that keep to these rules, and one draw needn't show every extreme that they name: `segment`: 0 marks the prompt, 1 the chosen response, 2 the rejected response; in order of position the prompt comes first, then the chosen, then the rejected response, each of them non-empty. `span_order`: a permutation of 0 to 31.
All inputs are finite; a program needn't handle non-finite values.
Results may differ from a plain program's by a relative error of at most 0.005.
Values may be sent and summed in bfloat16 or wider, within the bound.
No kernel may reach another device: no remote copies, remote signals or barrier semaphores. Data moves between devices by JAX's collectives and lax.ppermute only.
A program may use at most 64 MiB of HBM per device.

v0:
```python
import jax
import jax.numpy as jnp
from jax import lax
from jax.sharding import PartitionSpec as P

HEAD_DIM = 128


masked_score = -1e30


def block_mask(query_pos, query_seg, key_pos, key_seg):
    earlier = key_pos[None, :] <= query_pos[:, None]
    shared = (key_seg[None, :] == query_seg[:, None]) | (key_seg[None, :] == 0)
    return earlier & shared


def score_block(queries4, key_rows, scale_factor):
    key3 = key_rows.reshape(key_rows.shape[0], queries4.shape[1], queries4.shape[3])
    return (
        jnp.einsum("rgqd,ngd->gqrn", queries4, key3, preferred_element_type=jnp.float32)
        * scale_factor
    )


def stats_step(current, queries4, key_rows, visible, scale_factor):
    running_max, running_sum = current
    scores = jnp.where(visible, score_block(queries4, key_rows, scale_factor), masked_score)
    new_max = jnp.maximum(running_max, jnp.max(scores, axis=-1))
    weights = jnp.where(visible, jnp.exp(scores - new_max[..., None]), 0.0)
    return (new_max, running_sum * jnp.exp(running_max - new_max) + jnp.sum(weights, axis=-1))


def accumulate(current, key_rows, value_rows, visible, row_at, context):
    queries4, grads4, logsum, row_dot, scale_factor = context
    query_sum, key_sums, value_sums = current
    span_rows = key_rows.shape[0]
    key3 = key_rows.reshape(span_rows, queries4.shape[1], queries4.shape[3])
    value3 = value_rows.reshape(span_rows, queries4.shape[1], queries4.shape[3])
    scores = (
        jnp.einsum("rgqd,ngd->gqrn", queries4, key3, preferred_element_type=jnp.float32)
        * scale_factor
    )
    weights = jnp.where(visible, jnp.exp(scores - logsum[..., None]), 0.0)
    weights_low = weights.astype(jnp.bfloat16)
    value_term = jnp.einsum(
        "gqrn,rgqd->ngd", weights_low, grads4, preferred_element_type=jnp.float32
    )
    prob_grad = jnp.einsum("rgqd,ngd->gqrn", grads4, value3, preferred_element_type=jnp.float32)
    score_grad = (weights * (prob_grad - row_dot[..., None])).astype(jnp.bfloat16)
    query_term = (
        jnp.einsum("gqrn,ngd->rgqd", score_grad, key3, preferred_element_type=jnp.float32)
        * scale_factor
    )
    key_term = (
        jnp.einsum("gqrn,rgqd->ngd", score_grad, queries4, preferred_element_type=jnp.float32)
        * scale_factor
    )
    old_keys = lax.dynamic_slice_in_dim(key_sums, row_at, span_rows, 0)
    key_sums = lax.dynamic_update_slice_in_dim(key_sums, old_keys + key_term, row_at, 0)
    old_values = lax.dynamic_slice_in_dim(value_sums, row_at, span_rows, 0)
    value_sums = lax.dynamic_update_slice_in_dim(value_sums, old_values + value_term, row_at, 0)
    return (query_sum + query_term, key_sums, value_sums)


def over_blocks(advance, totals, row_count):
    block_rows = 512
    return lax.fori_loop(
        0,
        row_count // block_rows,
        lambda number, current: advance(current, number * block_rows, block_rows),
        totals,
    )


def reduce_keys(sums):
    return (
        lax.psum_scatter(sums[0], "ctx", scatter_dimension=0, tiled=True),
        lax.psum_scatter(sums[1], "ctx", scatter_dimension=0, tiled=True),
    )


def body(queries, keys, values, attn_out, out_grad, segment, span_order):
    ulysses_size = lax.axis_size("ulysses")
    ctx_size = lax.axis_size("ctx")
    exchanged = (
        lax.all_to_all(queries, "ulysses", split_axis=1, concat_axis=0, tiled=True),
        lax.all_to_all(attn_out, "ulysses", split_axis=1, concat_axis=0, tiled=True),
        lax.all_to_all(out_grad, "ulysses", split_axis=1, concat_axis=0, tiled=True),
        lax.all_to_all(keys, "ulysses", split_axis=1, concat_axis=0, tiled=True),
        lax.all_to_all(values, "ulysses", split_axis=1, concat_axis=0, tiled=True),
    )
    query_local, saved_local, grad_local, key_local, value_local = exchanged
    row_count = query_local.shape[0]
    kv_local = key_local.shape[1] // HEAD_DIM
    group_size = query_local.shape[1] // (kv_local * HEAD_DIM)
    shape4 = (row_count, kv_local, group_size, HEAD_DIM)
    queries4 = query_local.reshape(shape4)
    grads4 = grad_local.reshape(shape4)
    saved4 = saved_local.reshape(shape4)
    scale_factor = HEAD_DIM ** (-0.5)
    half_rows = row_count // 2
    block_rows = row_count // ulysses_size
    all_rows = row_count * ctx_size
    all_pos = (
        span_order[:, None] * half_rows + jnp.arange(half_rows, dtype=jnp.int32)[None, :]
    ).reshape(all_rows)
    all_seg = (
        segment.reshape(ulysses_size, ctx_size, block_rows).transpose(1, 0, 2).reshape(all_rows)
    )
    ctx_index = lax.axis_index("ctx")
    query_pos = lax.dynamic_slice_in_dim(all_pos, ctx_index * row_count, row_count)
    query_seg = lax.dynamic_slice_in_dim(all_seg, ctx_index * row_count, row_count)
    row_dot = jnp.einsum("rgqd,rgqd->gqr", grads4, saved4, preferred_element_type=jnp.float32)
    stat_shape = (kv_local, group_size, row_count)
    stats_init = (
        jnp.full(stat_shape, masked_score, jnp.float32),
        jnp.zeros(stat_shape, jnp.float32),
    )
    shard_piece = lax.all_gather(key_local, "ctx", axis=0, tiled=True)

    def advance(current, offset, span_rows):
        key_rows = lax.dynamic_slice_in_dim(shard_piece, offset, span_rows, 0)
        key_pos = lax.dynamic_slice_in_dim(all_pos, offset, span_rows)
        key_seg = lax.dynamic_slice_in_dim(all_seg, offset, span_rows)
        visible = block_mask(query_pos, query_seg, key_pos, key_seg)
        return stats_step(current, queries4, key_rows, visible, scale_factor)

    statistics = over_blocks(advance, stats_init, shard_piece.shape[0])
    logsum = statistics[0] + jnp.log(statistics[1])
    context = (queries4, grads4, logsum, row_dot, scale_factor)
    query_zero = jnp.zeros(shape4, jnp.float32)
    full_zero = jnp.zeros((all_rows, kv_local, HEAD_DIM), jnp.float32)
    key_piece = lax.all_gather(key_local, "ctx", axis=0, tiled=True)
    value_piece = lax.all_gather(value_local, "ctx", axis=0, tiled=True)

    def advance(current, offset, span_rows):
        key_rows = lax.dynamic_slice_in_dim(key_piece, offset, span_rows, 0)
        value_rows = lax.dynamic_slice_in_dim(value_piece, offset, span_rows, 0)
        key_pos = lax.dynamic_slice_in_dim(all_pos, offset, span_rows)
        key_seg = lax.dynamic_slice_in_dim(all_seg, offset, span_rows)
        visible = block_mask(query_pos, query_seg, key_pos, key_seg)
        return accumulate(current, key_rows, value_rows, visible, offset, context)

    query_sum, key_acc, value_acc = over_blocks(
        advance, (query_zero, full_zero, full_zero), key_piece.shape[0]
    )
    key_sum, value_sum = reduce_keys((key_acc, value_acc))
    query_out = query_sum.astype(jnp.bfloat16).reshape(row_count, kv_local * group_size * HEAD_DIM)
    key_out = key_sum.astype(jnp.bfloat16).reshape(row_count, kv_local * HEAD_DIM)
    value_out = value_sum.astype(jnp.bfloat16).reshape(row_count, kv_local * HEAD_DIM)
    returned_all = (
        lax.all_to_all(query_out, "ulysses", split_axis=0, concat_axis=1, tiled=True),
        lax.all_to_all(key_out, "ulysses", split_axis=0, concat_axis=1, tiled=True),
        lax.all_to_all(value_out, "ulysses", split_axis=0, concat_axis=1, tiled=True),
    )
    return (returned_all[0], returned_all[1], returned_all[2])


def solution(mesh):
    return jax.shard_map(
        body,
        mesh=mesh,
        in_specs=(
            P(("ulysses", "ctx"), None),
            P(("ulysses", "ctx"), None),
            P(("ulysses", "ctx"), None),
            P(("ulysses", "ctx"), None),
            P(("ulysses", "ctx"), None),
            P(),
            P(),
        ),
        out_specs=(
            P(("ulysses", "ctx"), None),
            P(("ulysses", "ctx"), None),
            P(("ulysses", "ctx"), None),
        ),
        check_vma=False,
    )
```

profile of v0, /device:TPU:0, one launch (start us, length us, event | category | flops | bytes accessed | tf_op | source)
XLA Modules:
  0.0 573.3 jit_solution(5427717440540506531)
XLA Ops:
  8.1 11.4 %all_to_all.143 = bf16[64,8,128]{2,0,1:T(8,128)(2,1)} all-to-all(bf16[64,8,128]{2,0,1:T(8,128)(2,1)S(1)} %copy_bitcast_fusion.6), channel_id=1, replica_groups=mesh['ulysses'=8,'ctx'=16] {'ulysses'}, dimensions={1} | all-to-all | bytes 262144 | tf_op jit(solution)/shard_map/all_to_all | solution.py:90
  21.1 3.4 all-to-all-start.2
  26.4 4.2 all-to-all-done.2
  30.6 3.5 all-to-all-start.1
  36.0 8.3 %all-to-all-done.1 = bf16[64,8,512]{2,0,1:T(8,128)(2,1)S(1)} async-done(((bf16[64,8,512]{2,0,1:T(8,128)(2,1)}), bf16[64,8,512]{2,0,1:T(8,128)(2,1)S(1)}, u32[]{:S(2)}, u32[]{:S(2)}) %all-to-all-start.1) | async-done | bytes 524320 | tf_op jit(solution)/shard_map/all_to_all | solution.py:87
  44.4 3.5 all-to-all-start.3
  48.7 9.4 %all-to-all-done.3 = bf16[64,8,512]{2,0,1:T(8,128)(2,1)S(1)} async-done(((bf16[64,8,512]{2,0,1:T(8,128)(2,1)}), bf16[64,8,512]{2,0,1:T(8,128)(2,1)S(1)}, u32[]{:S(2)}, u32[]{:S(2)}) %all-to-all-start.3) | async-done | bytes 524320 | tf_op jit(solution)/shard_map/all_to_all | solution.py:89
  58.1 3.5 all-to-all-start.4
  62.9 9.0 %all-to-all-done.4 = bf16[64,8,512]{2,0,1:T(8,128)(2,1)S(1)} async-done(((bf16[64,8,512]{2,0,1:T(8,128)(2,1)}), bf16[64,8,512]{2,0,1:T(8,128)(2,1)S(1)}, u32[]{:S(2)}, u32[]{:S(2)}) %all-to-all-start.4) | async-done | bytes 524320 | tf_op jit(solution)/shard_map/all_to_all | solution.py:88
  72.9 120.4 %while.34 = (s32[]{:T(128)}, f32[1,4,512]{2,1,0:T(4,128)S(1)}, f32[1,4,512]{2,1,0:T(4,128)S(1)}, s32[8192]{0:T(1024)S(1)}, s32[512]{0:T(512)S(1)}, /*index=5*/s3...) while((s32[]{:T(128)}, f32[1,4,512]{2,1,0:T(4,128)S(1)}, ...), condition=%wide.region_3.4_spmd.clone, body=%wide.region_0.3_spmd.clone.sunk | while | flops 277883392 | bytes 9954498 | solution.py:68
  73.4 3.7 fusion.89
  77.1 3.3 select_reduce_fusion.2
  81.0 3.7 fusion.89
  84.7 3.2 select_reduce_fusion.2
  88.5 3.7 fusion.89
  92.2 3.2 select_reduce_fusion.2
  96.0 3.7 fusion.89
  103.5 3.7 fusion.89
  107.2 3.3 select_reduce_fusion.2
  111.1 3.7 fusion.89
  114.8 3.2 select_reduce_fusion.2
  118.6 3.7 fusion.89
  122.4 3.2 select_reduce_fusion.2
  126.2 3.7 fusion.89
  129.9 3.2 select_reduce_fusion.2
  133.7 3.7 fusion.89
  137.4 3.2 select_reduce_fusion.2
  141.2 3.7 fusion.89
  144.9 3.2 select_reduce_fusion.2
  148.7 3.7 fusion.89
  152.4 3.2 select_reduce_fusion.2
  156.2 3.7 fusion.89
  160.0 3.2 select_reduce_fusion.2
  163.8 3.7 fusion.89
  167.5 3.2 select_reduce_fusion.2
  171.3 3.7 fusion.89
  175.0 3.2 select_reduce_fusion.2
  178.8 3.7 fusion.89
  182.5 3.2 select_reduce_fusion.2
  186.3 3.7 fusion.89
  190.0 3.2 select_reduce_fusion.2
  197.9 198.4 %while.35 = (s32[]{:T(128)}, f32[512,1,4,128]{0,3,2,1:T(8,128)}, f32[8192,1,128]{2,0,1:T(8,128)}, f32[8192,1,128]{2,0,1:T(8,128)}, bf16[8192,128]{1,0:T(8,128)(2...) while((s32[]{:T(128)}, f32[512,1,4,128]{0,3,2,1:T(8,128)}, ...), condition=%wide.region_5.6_spmd.clone, body=%wide.region_4.5_spmd.clone.sunk | while | flops 1354695168 | bytes 25339128 | solution.py:68
  398.9 3.5 all-to-all-start.5
  402.4 71.1 %reduce-scatter.5.cloned.1.call-done = f32[512,1,128]{2,0,1:T(8,128)} async-done(((f32[8192,1,128]{2,0,1:T(8,128)}), f32[512,1,128]{2,0,1:T(8,128)}) %reduce-scatter.5.cloned.1.call-update) | async-done | bytes 262160 | tf_op jit(solution)/shard_map/reduce_scatter | solution.py:79
  475.1 4.4 all-to-all-start.7
  480.3 73.6 %reduce-scatter.3.cloned.1.call-done = f32[512,1,128]{2,0,1:T(8,128)} async-done(((f32[8192,1,128]{2,0,1:T(8,128)}), f32[512,1,128]{2,0,1:T(8,128)}) %reduce-scatter.3.cloned.1.call-update) | async-done | bytes 262160 | tf_op jit(solution)/shard_map/reduce_scatter | solution.py:78
  555.5 4.5 all-to-all-start.6
  560.7 5.5 all-to-all-done.6
  (284 shorter events, 231.6 us)
Async XLA Ops:
  7.2 0.9 copy-start
  7.2 40.7 %copy-start.2 = (bf16[64,4096]{1,0:T(8,128)(2,1)S(1)}, bf16[64,4096]{1,0:T(8,128)(2,1)}, u32[]{:S(2)}) copy-start(bf16[64,4096]{1,0:T(8,128)(2,1)} %param.14) | copy-start | bytes 1572868
  7.2 54.5 %copy-start.4 = (s32[8192]{0:T(1024)S(1)}, s32[8192]{0:T(1024)}, u32[]{:S(2)}) copy-start(s32[8192]{0:T(1024)} %param.16) | copy-start | bytes 98308
  7.2 54.7 %copy-start.5 = (s32[32]{0:T(128)S(1)}, s32[32]{0:T(128)}, u32[]{:S(2)}) copy-start(s32[32]{0:T(128)} %param.17) | copy-start | bytes 388
  7.2 65.7 %all-gather.3.cloned.1.call-start = ((), (), s32[]{:S(2)}) async-start(), calls=%async_computation.10 | async-start | bytes 2228224 | tf_op jit(solution)/shard_map/all_gather | solution.py:134
  21.1 9.4 %all-to-all-start.2 = ((bf16[64,8,128]{2,0,1:T(8,128)(2,1)}), bf16[64,8,128]{2,0,1:T(8,128)(2,1)S(1)}, u32[]{:S(2)}, u32[]{:S(2)}) async-start(bf16[64,8,128]{2,0,1:T(8,128)(2,1)} %copy_bitcast_fusion.5), calls=%async_computation.2 | async-start | bytes 262144 | tf_op jit(solution)/shard_map/all_to_all | solution.py:91
  30.6 31.6 %copy-start.3 = (bf16[64,8,128]{2,0,1:T(8,128)(2,1)}, bf16[64,8,128]{2,0,1:T(8,128)(2,1)S(1)}, u32[]{:S(2)}) copy-start(bf16[64,8,128]{2,0,1:T(8,128)(2,1)S(1)} %all-to-all-done.2) | copy-start | bytes 393220
  30.6 13.8 %all-to-all-start.1 = ((bf16[64,8,512]{2,0,1:T(8,128)(2,1)}), bf16[64,8,512]{2,0,1:T(8,128)(2,1)S(1)}, u32[]{:S(2)}, u32[]{:S(2)}) async-start(bf16[64,8,512]{2,0,1:T(8,128)(2,1)} %bitcast.199), calls=%async_computation.1 | async-start | bytes 1048576 | tf_op jit(solution)/shard_map/all_to_all | solution.py:87
  44.4 13.8 %all-to-all-start.3 = ((bf16[64,8,512]{2,0,1:T(8,128)(2,1)}), bf16[64,8,512]{2,0,1:T(8,128)(2,1)S(1)}, u32[]{:S(2)}, u32[]{:S(2)}) async-start(bf16[64,8,512]{2,0,1:T(8,128)(2,1)} %bitcast.198), calls=%async_computation.3 | async-start | bytes 1048576 | tf_op jit(solution)/shard_map/all_to_all | solution.py:89
  58.1 13.8 %all-to-all-start.4 = ((bf16[64,8,512]{2,0,1:T(8,128)(2,1)}), bf16[64,8,512]{2,0,1:T(8,128)(2,1)S(1)}, u32[]{:S(2)}, u32[]{:S(2)}) async-start(bf16[64,8,512]{2,0,1:T(8,128)(2,1)} %bitcast.197), calls=%async_computation.4 | async-start | bytes 1048576 | tf_op jit(solution)/shard_map/all_to_all | solution.py:88
  61.6 131.7 %all-gather.5.cloned.1.call-start = ((), (), s32[]{:S(2)}) async-start(), calls=%async_computation.11 | async-start | bytes 2228224 | tf_op jit(solution)/shard_map/all_gather | solution.py:135
  62.4 411.1 %reduce-scatter.5.cloned.1.call-start = ((), (), s32[]{:S(2)}) async-start(), calls=%async_computation.13 | async-start | bytes 4456448 | tf_op jit(solution)/shard_map/reduce_scatter | solution.py:79
  396.3 1.2 copy-start.1
  396.3 157.6 %reduce-scatter.3.cloned.1.call-start = ((), (), s32[]{:S(2)}) async-start(), calls=%async_computation.12 | async-start | bytes 4456448 | tf_op jit(solution)/shard_map/reduce_scatter | solution.py:78
  398.9 76.2 %all-to-all-start.5 = ((bf16[8,64,512]{2,1,0:T(8,128)(2,1)}), bf16[8,64,512]{2,1,0:T(8,128)(2,1)S(1)}, u32[]{:S(2)}, u32[]{:S(2)}) async-start(bf16[8,64,512]{2,1,0:T(8,128)(2,1)} %all_to_all.123), calls=%async_computation.5 | async-start | bytes 1048576 | tf_op jit(solution)/shard_map/all_to_all | solution.py:153
  475.1 80.4 %all-to-all-start.7 = ((bf16[8,64,128]{2,1,0:T(8,128)(2,1)}), bf16[8,64,128]{2,1,0:T(8,128)(2,1)S(1)}, u32[]{:S(2)}, u32[]{:S(2)}) async-start(bf16[8,64,128]{2,1,0:T(8,128)(2,1)} %bitcast.14), calls=%async_computation.9 | async-start | bytes 262144 | tf_op jit(solution)/shard_map/all_to_all | solution.py:155
  555.5 10.6 %all-to-all-start.6 = ((bf16[8,64,128]{2,1,0:T(8,128)(2,1)}), bf16[8,64,128]{2,1,0:T(8,128)(2,1)S(1)}, u32[]{:S(2)}, u32[]{:S(2)}) async-start(bf16[8,64,128]{2,1,0:T(8,128)(2,1)} %bitcast.12), calls=%async_computation.7 | async-start | bytes 262144 | tf_op jit(solution)/shard_map/all_to_all | solution.py:154
Sparse Core Ops, SparseCore 0:
  19.7 44.2 all-gather.2
  66.7 45.0 all-gather.4
  396.4 77.0 reduce-scatter.4
  477.0 76.8 reduce-scatter.2
where the time goes:
time: 578 us; the launch traced here: 573 us
  matrix products  249 us (43%)
  waiting for transfers between devices  182 us (31%)
  other arithmetic  70 us (12%)
  starting transfers between devices  26.4 us (5%)
  local copies, waits for them, and re-layouts  19.2 us (3%)
  between operations  14 us (2%)
  blocking collectives  11.4 us (2%)
    reduce_scatter x1, waiting for transfers between devices, reduce_keys(): lax.psum_scatter(sums[0], 'ctx', scatter_dimension=0, tiled=True)  73.6 us
    reduce_scatter x1, waiting for transfers between devices, reduce_keys(): lax.psum_scatter(sums[1], 'ctx', scatter_dimension=0, tiled=True)  71.1 us
    dot_general x16, matrix products, score_block(): jnp.einsum('rgqd,ngd->gqrn', queries4, key3, preferred_element_type=jnp.f...  59.3 us
    reduce_sum x16, other arithmetic, stats_step(): jnp.sum(weights, axis=-1)  51.9 us
    dot_general x16, matrix products, accumulate(): jnp.einsum('gqrn,ngd->rgqd', score_grad, key3, preferred_element_type=jnp...  44.6 us
    dot_general x16, matrix products, accumulate(): jnp.einsum('gqrn,rgqd->ngd', weights_low, grads4, preferred_element_type=...  42.6 us
    dot_general x16, matrix products, accumulate(): jnp.einsum('rgqd,ngd->gqrn', grads4, value3, preferred_element_type=jnp.f...  39.2 us
    dot_general x16, matrix products, accumulate(): jnp.einsum('gqrn,rgqd->ngd', score_grad, queries4, preferred_element_type...  37.9 us
  transfers between devices with their start and end apart: 11, of which 7 were waited for; matrix products, arithmetic and copies ran while one was open for 23% of the time, Pallas kernels for 0%

commit v1 on v0

v1 whole, which is shorter than its diff:
```python
import math

import jax
import jax.numpy as jnp
from jax import lax
from jax.experimental import pallas as pl
from jax.experimental.pallas import tpu as pltpu
from jax.sharding import Mesh, PartitionSpec as P

D = 128
G = 4
R = 64
HR = R // 2
SPAN = 256
SPANS = 32
KB = 2 * SPAN
QR = G * HR
C = 2 * QR
NC = 8
W = 4
WM = 2
SCALE = D**-0.5
EXP_SCALE = SCALE * math.log2(math.e)
HIDDEN = -1e30
LARGE = 2.0**90
F32 = jnp.float32
BF16 = jnp.bfloat16
AXES = ("z", "core", "xh", "xl", "y")
SPREAD = ("xh", "xl", "z")
NT_DIMS = (((1,), (1,)), ((), ()))

OWN, NEAR, FAR = (0,), (1, 3), (2,)


def spread_to(g, xl):
    return (g // 4 * 2 + xl) * 4 + g % 4


def head_columns(g, h):
    return slice((g * G + h) * D, (g * G + h + 1) * D)


def pack_kv_kernel(keys, values, segment, out, counts):
    counts[0] = jnp.sum((segment[...] == 0).astype(jnp.int32))
    counts[1] = jnp.sum((segment[...] != 2).astype(jnp.int32))
    for g in range(8):
        for xl in range(2):
            out[spread_to(g, xl), :R] = keys[:, g * D : (g + 1) * D]
            out[spread_to(g, xl), R:] = values[:, g * D : (g + 1) * D]


def pack_q_kernel(queries, saved, grads, after, out):
    del after
    ones = jnp.ones((8, D), BF16)
    row = lax.broadcasted_iota(jnp.int32, (16, D), 0)
    for g in range(8):
        for half in range(2):
            dest = spread_to(g, half)
            rows = slice(half * HR, (half + 1) * HR)
            prods = []
            for h in range(G):
                cols = head_columns(g, h)
                grad = grads[rows, cols]
                out[dest, h * HR : (h + 1) * HR] = queries[rows, cols]
                out[dest, QR + h * HR : QR + (h + 1) * HR] = grad
                prods.append(grad.astype(F32) * saved[rows, cols].astype(F32))
            prod = jnp.concatenate(prods, axis=0)
            high = prod.astype(BF16)
            low = (prod - high.astype(F32)).astype(BF16)
            dot = lax.dot_general(ones, high, NT_DIMS, preferred_element_type=F32)
            dot = dot + lax.dot_general(ones, low, NT_DIMS, preferred_element_type=F32)
            both = jnp.concatenate([dot, dot], axis=0)
            rounded = both.astype(BF16).astype(F32)
            out[dest, 2 * QR :] = jnp.where(row == 0, rounded, both - rounded).astype(BF16)


def span_id(xh, xl, y, zh):
    return ((xh * 2 + xl) * 4 + y) * 2 + zh


class Place:
    def __init__(self, order, counts):
        self.order = order
        self.n0, self.n1 = counts[0], counts[1]
        self.xl = lax.axis_index("xl")
        self.y = lax.axis_index("y")
        self.core = lax.axis_index("core")

    def span_of(self, c):
        return self.order[span_id(c // 4, c // 2 % 2, self.y, c % 2)]


class Group:
    def __init__(self, place, distances, base, table, below):
        self.place, self.base, self.table, self.below = place, base, table, below
        self.own = 0 in distances
        self.entries = [
            (dy, xh, xl, zh)
            for dy in distances
            for xh in range(2)
            for xl in range(2)
            for zh in range(2)
        ]

        def clear(i, carry):
            below[i] = 0
            return carry

        lax.fori_loop(0, SPANS + 1, clear, 0)
        spans = []
        for dy, xh, xl, zh in self.entries:
            span = place.order[span_id(xh, xl, place.y ^ dy, zh)]
            below[span] = 1
            spans.append(span)

        def count(i, total):
            here = below[i]
            below[i] = total

            @pl.when(here == 1)
            def _():
                table[base + total] = i

            return total + here

        lax.fori_loop(0, SPANS + 1, count, jnp.int32(0))
        self.slots = [base + below[span] for span in spans]

    def copies(self, pieces, part, dst, sem):
        made = []
        for (dy, xh, xl, zh), slot in zip(self.entries, self.slots):
            for from_core, arrays in zip((self.place.core, 1 - self.place.core), pieces[dy]):
                row = (xl * 2 + zh) * 2
                if len(arrays) == 2:
                    rows = arrays[xh].at[pl.ds(row, 2)]
                else:
                    rows = arrays[0].at[pl.ds(xh * 8 + row, 2)]
                made.append(
                    pltpu.make_async_copy(
                        rows.at[:, pl.ds(part * R, R)],
                        dst.at[slot, :, from_core, :, pl.ds(0, D)],
                        sem,
                    )
                )
        return made

    def put_sums(self, dy, xh, array, from_core, at_xh, dk_s, dv_s):
        for (entry_dy, entry_xh, xl, zh), slot in zip(self.entries, self.slots):
            if entry_dy == dy and entry_xh == xh:
                row = (((xh * 2 if at_xh else 0) + xl) * 2 + zh) * 2
                array[row : row + 2, :R] = (dk_s[slot, :, from_core] * SCALE).astype(BF16)
                array[row : row + 2, R:] = dv_s[slot, :, from_core].astype(BF16)


class Lists:
    def __init__(self, place, table, refs):
        self.place, self.table = place, table
        self.plain_c, self.plain_b, self.masked_c, self.masked_b = refs
        self.n_plain = self.n_masked = jnp.int32(0)

    def add(self, group):
        place, base = self.place, group.base // 2
        n0, n1 = place.n0, place.n1
        if group.own:
            self.n_masked = jnp.int32(NC)

        def chunk(c, sizes):
            n_plain, n_masked = sizes
            span_q = place.span_of(c)
            first = span_q * SPAN
            has_second = first + (SPAN - 1) >= n1
            all_second = first >= n1
            before = group.below[span_q]
            n_full = before // 2
            hi = (group.below[(n1 + (SPAN - 1)) // SPAN] + 1) // 2
            hi = jnp.minimum(jnp.where(has_second, hi, 0), n_full)
            lo = jnp.minimum(jnp.where(has_second, group.below[n0 // SPAN] // 2, 0), hi)
            skip_at = (group.below[(n0 + (SPAN - 1)) // SPAN] + 1) // 2
            skip_at = jnp.where(all_second, skip_at, hi)
            skip_to = jnp.where(all_second, group.below[n1 // SPAN] // 2, 0)

            def put_plain(b, n):
                self.plain_c[n] = c
                self.plain_b[n] = base + b
                return n + 1

            def put_masked(b, n):
                hidden = (b >= skip_at) & (b < skip_to)
                self.masked_c[n] = c
                self.masked_b[n] = base + b
                return jnp.where(hidden, n, n + 1)

            n_plain = lax.fori_loop(0, lo, put_plain, n_plain)
            n_plain = lax.fori_loop(hi, n_full, put_plain, n_plain)
            n_masked = lax.fori_loop(lo, hi, put_masked, n_masked)
            if group.own:
                self.masked_c[c] = c
                self.masked_b[c] = base + n_full
            else:
                self.masked_c[n_masked] = c
                self.masked_b[n_masked] = base + n_full
                n_masked = n_masked + before % 2
            return n_plain, n_masked

        self.n_plain, self.n_masked = lax.fori_loop(0, NC, chunk, (self.n_plain, self.n_masked))
        for i in range(W - 1):
            self.plain_c[self.n_plain + i] = NC
            self.plain_b[self.n_plain + i] = 0
        for i in range(WM - 1):
            self.masked_c[self.n_masked + i] = NC
            self.masked_b[self.n_masked + i] = 0
        self.n_plain = (self.n_plain + (W - 1)) // W * W
        self.n_masked = (self.n_masked + (WM - 1)) // WM * WM

    def each(self, step, first_masked=0):
        def masked(i, carry):
            at = [WM * i + k for k in range(WM)]
            step([(self.masked_c[n], self.masked_b[n]) for n in at], True)
            return carry

        def plain(i, carry):
            at = [W * i + k for k in range(W)]
            step([(self.plain_c[n], self.plain_b[n]) for n in at], False)
            return carry

        lax.fori_loop(first_masked // WM, self.n_masked // WM, masked, 0)
        lax.fori_loop(0, self.n_plain // W, plain, 0)

    def one_by_one(self, step):
        def masked(n, carry):
            @pl.when(self.masked_c[n] < NC)
            def _():
                step(self.masked_c[n], self.masked_b[n])

            return carry

        def plain(n, carry):
            @pl.when(self.plain_c[n] < NC)
            def _():
                step(self.plain_c[n], self.plain_b[n])

            return carry

        lax.fori_loop(0, self.n_masked, masked, 0)
        lax.fori_loop(0, self.n_plain, plain, 0)

    def seen(self, c, b):
        place = self.place
        lane = lax.broadcasted_iota(jnp.int32, (1, C), 1)
        start = place.span_of(jnp.minimum(c, NC - 1)) * SPAN + place.core * R + place.xl * HR
        query_pos = start + (lane // QR) * (2 * R) + lane % HR
        row = lax.broadcasted_iota(jnp.int32, (KB, 1), 0)
        start = jnp.where(row < SPAN, self.table[2 * b], self.table[2 * b + 1] - 1)
        key_pos = start * SPAN + row
        low = jnp.where(query_pos >= place.n1, place.n0, place.n1)
        return (key_pos <= query_pos) & ((key_pos < low) | (key_pos >= place.n1))


def block_of(ref, b):
    return ref[pl.ds(2 * b, 2)].reshape(KB, 2 * D)


def keys_of(k_s, b):
    return k_s[pl.ds(2 * b, 2), :, :, :, :D].reshape(KB, D)


def add_up(weights):
    return jnp.sum(weights.reshape(KB // 8, 8, C), axis=0)


def put_under(ref, c, *rows):
    number = lax.broadcasted_iota(jnp.int32, (D, C), 0)
    block = jnp.zeros((D, C), F32)
    for i, values in enumerate(rows):
        block = jnp.where(number == i, values, block)
    ref[c, D:] = block.astype(BF16)


def put_beside(*refs):
    beside = lax.broadcasted_iota(jnp.int32, (1, 1, 1, 1, D), 4) < 3
    beside = jnp.broadcast_to(beside.astype(F32), (1, 2, 2, R, D)).astype(BF16)

    def step(i, carry):
        for ref in refs:
            ref[pl.ds(i, 1), :, :, :, D:] = beside
        return carry

    lax.fori_loop(0, refs[0].shape[0], step, 0)


def put_empty_chunk(qa_s):
    qa_s[NC, :D] = jnp.zeros((D, C), BF16)
    put_under(qa_s, NC, jnp.full((1, C), HIDDEN, F32))


def weights_of(lists, c, b, masked, k_s, qa_s):
    scores = jnp.dot(block_of(k_s, b), qa_s[c], preferred_element_type=F32)
    if masked:
        scores = jnp.where(lists.seen(c, b), scores, HIDDEN)
    return jnp.exp2(scores * EXP_SCALE)


def add_stats(lists, k_s, qa_s, l_s, first_masked=0):
    def step(items, masked):
        parts = [add_up(weights_of(lists, c, b, masked, k_s, qa_s)) for c, b in items]
        for (c, b), part in zip(items, parts):
            l_s[c] += part

    lists.each(step, first_masked)


def careful_stats(lists, k_s, qa_s, m_s, l_s):
    def step(c, b):
        scores = jnp.dot(keys_of(k_s, b), qa_s[c, :D], preferred_element_type=F32) * EXP_SCALE
        scores = jnp.where(lists.seen(c, b), scores, HIDDEN)
        old = m_s[c]
        top = jnp.maximum(old, jnp.max(scores, axis=0, keepdims=True))
        l_s[c] = l_s[c] * jnp.exp2(old - top) + add_up(jnp.exp2(scores - top))
        m_s[c] = top

    lists.one_by_one(step)


def stats_kernel(
    order, counts, qpay, own, own_o, near_1, near_1o, near_3, near_3o,
    m_out, l_out, qt_out, g_out, ga_out,
    table, below_0, below_1, plain_c, plain_b, masked_c, masked_b,
    q_s, d_s, k_s, qa_s, l_s, sem, grad_sem,
):
    place = Place(order, counts)
    copies = []
    grad_copies = []
    for s in range(2 * NC):
        rows = pl.ds((s % 2) * QR, QR)
        copies.append(
            pltpu.make_async_copy(qpay.at[s, pl.ds(0, QR)], q_s.at[s // 2, rows], sem)
        )
        grad_copies.append(
            pltpu.make_async_copy(qpay.at[s, pl.ds(QR, QR)], g_out.at[s // 2, rows], grad_sem)
        )
    grad_copies.append(pltpu.make_async_copy(qpay.at[:, pl.ds(2 * QR, 16)], d_s, grad_sem))
    for copy in copies:
        copy.start()
    pieces = {0: ([own], [own_o]), 1: ([near_1], [near_1o]), 3: ([near_3], [near_3o])}
    groups = [Group(place, OWN, 0, table, below_0), Group(place, NEAR, 8, table, below_1)]
    for group in groups:
        key_copies = group.copies(pieces, 0, k_s, sem)
        for copy in key_copies:
            copy.start()
        copies += key_copies
    for copy in grad_copies:
        copy.start()
    put_beside(k_s)
    put_empty_chunk(qa_s)
    l_s[NC] = jnp.zeros((8, C), F32)
    lists = Lists(place, table, (plain_c, plain_b, masked_c, masked_b))
    for group in groups:
        lists.add(group)
    for copy in copies:
        copy.wait()

    def turn(c, carry):
        turned = q_s[c].T
        qa_s[c, :D] = turned
        qt_out[c] = turned
        return carry

    lax.fori_loop(0, NC, turn, 0)

    def diagonal_step(i, carry):
        for c in [2 * i + k for k in range(2)]:
            b = masked_b[c]
            scores = jnp.dot(keys_of(k_s, b), qa_s[c, :D], preferred_element_type=F32)
            scores = jnp.where(lists.seen(c, b), scores, HIDDEN)
            top = jnp.max(scores, axis=0, keepdims=True).astype(BF16).astype(F32)
            put_under(qa_s, c, -top)
            m_out[c] = top * EXP_SCALE
            l_s[c] = add_up(jnp.exp2((scores - top) * EXP_SCALE))
        return carry

    lax.fori_loop(0, NC // 2, diagonal_step, 0)
    add_stats(lists, k_s, qa_s, l_s, NC)

    @pl.when(jnp.logical_not(jnp.max(l_s[...]) < LARGE))
    def _():
        for c in range(NC):
            m_out[c] = jnp.full((1, C), HIDDEN, F32)
            l_s[c] = jnp.zeros((8, C), F32)
        careful_stats(lists, k_s, qa_s, m_out, l_s)

    for c in range(NC):
        l_out[c] = l_s[c]

    for copy in grad_copies:
        copy.wait()

    def turn_grads(c, carry):
        ga_out[c, :D] = g_out[c].T
        halves = [d_s[2 * c + half].astype(F32) for half in range(2)]
        put_under(
            ga_out,
            c,
            -jnp.concatenate([half[0:1] for half in halves], axis=1),
            -jnp.concatenate([half[1:2] for half in halves], axis=1),
        )
        return carry

    lax.fori_loop(0, NC, turn_grads, 0)


def query_copies(qpay, qt, q_s, qa_s, sem):
    made = [pltpu.make_async_copy(qt, qa_s.at[pl.ds(0, NC), pl.ds(0, D)], sem)]
    for s in range(2 * NC):
        rows = pl.ds((s % 2) * QR, QR)
        made.append(pltpu.make_async_copy(qpay.at[s, pl.ds(0, QR)], q_s.at[s // 2, rows], sem))
    return made


def grad_pass(lists, logsum, q_s, g_in, ga_in, k_s, v_s, kt_s, qa_s, dk_s, dv_s, dq_s):
    def turn(b, carry):
        kt_s[b] = keys_of(k_s, b).T
        return carry

    lax.fori_loop(0, kt_s.shape[0], turn, 0)

    def put_logsum(c, carry):
        rest = logsum[c] * (1.0 / EXP_SCALE)
        rows = []
        for _ in range(3):
            part = rest.astype(BF16).astype(F32)
            rows.append(-part)
            rest = rest - part
        put_under(qa_s, c, *rows)
        return carry

    lax.fori_loop(0, NC, put_logsum, 0)

    def step(items, masked):
        weights = [weights_of(lists, c, b, masked, k_s, qa_s) for c, b in items]
        of = [jnp.minimum(c, NC - 1) for c, b in items]
        above = [
            jnp.dot(block_of(v_s, b), ga_in[c], preferred_element_type=F32)
            for c, (_, b) in zip(of, items)
        ]
        score_grads = [(w * p).astype(BF16) for w, p in zip(weights, above)]
        for c, (_, b), w, score_grad in zip(of, items, weights, score_grads):
            for ref, term in (
                (dv_s, jnp.dot(w.astype(BF16), g_in[c], preferred_element_type=F32)),
                (dk_s, jnp.dot(score_grad, q_s[c], preferred_element_type=F32)),
            ):
                ref[pl.ds(2 * b, 2)] += term.reshape(2, 2, 2, R, D)
            dq_s[c] += jnp.dot(kt_s[b], score_grad, preferred_element_type=F32)

    lists.each(step)


def far_near_kernel(
    order, counts, m_in, l_in, g_in, ga_in,
    qpay, qt, far_a, far_b, far_ao, far_bo, near_1, near_1o, near_3, near_3o,
    logsum, dq, far_give, give_1, give_3, sum_a, sum_b, sum_1, sum_3,
    table, below_0, below_1, plain_c, plain_b, masked_c, masked_b,
    q_s, k_s, v_s, kt_s, qa_s, dk_s, dv_s, m_s, l_s, sem, value_sem,
):
    place = Place(order, counts)
    copies = query_copies(qpay, qt, q_s, qa_s, sem)
    for copy in copies:
        copy.start()
    pieces = {
        2: ([far_a, far_b], [far_ao, far_bo]),
        1: ([near_1], [near_1o]),
        3: ([near_3], [near_3o]),
    }
    groups = [Group(place, FAR, 0, table, below_0), Group(place, NEAR, 8, table, below_1)]
    value_copies = []
    for group in groups:
        key_copies = group.copies(pieces, 0, k_s, sem)
        for copy in key_copies:
            copy.start()
        copies += key_copies
    for group in groups:
        value_copies += group.copies(pieces, 1, v_s, value_sem)
    for copy in value_copies:
        copy.start()
    put_beside(k_s, v_s)
    put_empty_chunk(qa_s)
    for ref in (dk_s, dv_s, dq):
        ref[...] = jnp.zeros_like(ref)

    def take(c, carry):
        top = (m_in[c] * (1.0 / EXP_SCALE)).astype(BF16).astype(F32)
        put_under(qa_s, c, -top)
        m_s[c] = top * EXP_SCALE
        l_s[c] = l_in[c] * jnp.exp2(m_in[c] - top * EXP_SCALE)
        return carry

    lax.fori_loop(0, NC, take, 0)
    l_s[NC] = jnp.zeros((8, C), F32)
    lists = Lists(place, table, (plain_c, plain_b, masked_c, masked_b))
    lists.add(groups[0])
    for copy in copies:
        copy.wait()
    add_stats(lists, k_s, qa_s, l_s)

    @pl.when(jnp.logical_not(jnp.max(l_s[...]) < LARGE))
    def _():
        for c in range(NC):
            m_s[c] = m_in[c]
            l_s[c] = l_in[c]
        careful_stats(lists, k_s, qa_s, m_s, l_s)

    for c in range(NC):
        logsum[c] = m_s[c] + jnp.log2(jnp.sum(l_s[c], axis=0, keepdims=True))
    lists.add(groups[1])
    for copy in value_copies:
        copy.wait()
    grad_pass(lists, logsum, q_s, g_in, ga_in, k_s, v_s, kt_s, qa_s, dk_s, dv_s, dq)
    far, near = groups
    far.put_sums(2, 0, sum_a, place.core, False, dk_s, dv_s)
    far.put_sums(2, 1, sum_b, place.core, False, dk_s, dv_s)
    for xh in range(2):
        far.put_sums(2, xh, far_give, 1 - place.core, True, dk_s, dv_s)
        for dy, keep, give in ((1, sum_1, give_1), (3, sum_3, give_3)):
            near.put_sums(dy, xh, keep, place.core, True, dk_s, dv_s)
            near.put_sums(dy, xh, give, 1 - place.core, True, dk_s, dv_s)


def own_kernel(
    order, counts, logsum, dq_in, g_in, ga_in, after, qpay, qt, own, own_o,
    dq_out, keep, give,
    table, below_0, plain_c, plain_b, masked_c, masked_b,
    q_s, k_s, v_s, kt_s, qa_s, dk_s, dv_s, dq_s, sem,
):
    del after
    place = Place(order, counts)
    copies = query_copies(qpay, qt, q_s, qa_s, sem)
    group = Group(place, OWN, 0, table, below_0)
    pieces = {0: ([own], [own_o])}
    copies += group.copies(pieces, 0, k_s, sem) + group.copies(pieces, 1, v_s, sem)
    for copy in copies:
        copy.start()
    put_beside(k_s, v_s)
    put_empty_chunk(qa_s)
    for ref in (dk_s, dv_s):
        ref[...] = jnp.zeros_like(ref)
    dq_s[...] = dq_in[...]
    lists = Lists(place, table, (plain_c, plain_b, masked_c, masked_b))
    lists.add(group)
    for copy in copies:
        copy.wait()
    grad_pass(lists, logsum, q_s, g_in, ga_in, k_s, v_s, kt_s, qa_s, dk_s, dv_s, dq_s)
    for xh in range(2):
        group.put_sums(0, xh, keep, place.core, True, dk_s, dv_s)
        group.put_sums(0, xh, give, 1 - place.core, True, dk_s, dv_s)

    def finish(c, carry):
        dq = (dq_s[c] * SCALE).T.astype(BF16)
        dq_out[2 * c] = dq[:QR]
        dq_out[2 * c + 1] = dq[QR:]
        return carry

    lax.fori_loop(0, NC, finish, 0)


def far_sum_kernel(sum_a, sum_b, got, out_a, out_b, after):
    out_a[...] = (sum_a[...].astype(F32) + got[:8].astype(F32)).astype(BF16)
    out_b[...] = (sum_b[...].astype(F32) + got[8:].astype(F32)).astype(BF16)
    after[...] = jnp.zeros_like(after)


def near_sum_kernel(sum_1, got_1, sum_3, got_3, from_1, from_3, out_1, out_3):
    for rows, with_from in ((slice(0, 8), 3), (slice(8, 16), 1)):
        for number, keep, got, came, out in (
            (1, sum_1, got_1, from_3, out_1),
            (3, sum_3, got_3, from_1, out_3),
        ):
            total = keep[rows].astype(F32) + got[rows].astype(F32)
            if number == with_from:
                total = total + came[...].astype(F32)
            out[rows] = total.astype(BF16)


def last_sum_kernel(keep, got, near_1, near_3, dq, sums, query_grad):
    total = keep[...].astype(F32) + got[...].astype(F32)
    total = total + (near_1[...].astype(F32) + near_3[...].astype(F32))
    sums[...] = total.astype(BF16)
    for g in range(8):
        for half in range(2):
            rows = slice(half * HR, (half + 1) * HR)
            for h in range(G):
                query_grad[rows, head_columns(g, h)] = dq[spread_to(g, half), h * HR : (h + 1) * HR]


def unpack_kernel(got, key_grad, value_grad):
    for g in range(8):
        for start, out in ((0, key_grad), (R, value_grad)):
            total = got[spread_to(g, 0), start : start + R].astype(F32)
            total = total + got[spread_to(g, 1), start : start + R].astype(F32)
            out[:, g * D : (g + 1) * D] = total.astype(BF16)


def bf16(*shape):
    return jax.ShapeDtypeStruct(shape, BF16)


def f32(*shape):
    return jax.ShapeDtypeStruct(shape, F32)


def on_vmem(kernel, outs, *args):
    return pl.pallas_call(
        kernel,
        out_shape=outs,
        compiler_params=pltpu.CompilerParams(vmem_limit_bytes=16 << 20),
    )(*args)


IN_SMEM = pl.BlockSpec(memory_space=pltpu.SMEM)
IN_VMEM = pl.BlockSpec(memory_space=pltpu.VMEM)
ANYWHERE = pl.BlockSpec(memory_space=pl.ANY)


def on_group(kernel, outs, spans, groups, scratch, tables, held, anywhere, products):
    smem = [pltpu.SMEM((spans,), jnp.int32)] + [pltpu.SMEM((SPANS + 1,), jnp.int32)] * groups
    smem += [pltpu.SMEM((NC * (spans // 2 + 1) + 4 * W,), jnp.int32)] * 4
    work = products * NC * C * spans * SPAN * D * 2 // 3
    return pl.pallas_call(
        kernel,
        out_shape=outs,
        in_specs=[IN_SMEM] * 2 + [IN_VMEM] * len(held) + [ANYWHERE] * len(anywhere),
        scratch_shapes=smem + scratch,
        compiler_params=pltpu.CompilerParams(vmem_limit_bytes=44 << 20),
        cost_estimate=pl.CostEstimate(
            flops=work, bytes_accessed=4 << 20, transcendentals=NC * C * spans * SPAN // 3
        ),
    )(*tables, *held, *anywhere)


def exchange(array):
    return lax.all_to_all(array, SPREAD, split_axis=0, concat_axis=0, tiled=True)


def flip(array):
    return lax.ppermute(array, "core", [(0, 1), (1, 0)])


def swap(array, distance):
    return lax.ppermute(array, "y", [(i, i ^ distance) for i in range(4)])


def body(queries, keys, values, attn_out, out_grad, segment, span_order):
    kv_packed, counts = pl.pallas_call(
        pack_kv_kernel,
        out_shape=[bf16(16, 2 * R, D), jax.ShapeDtypeStruct((2,), jnp.int32)],
        out_specs=[IN_VMEM, IN_SMEM],
        compiler_params=pltpu.CompilerParams(vmem_limit_bytes=16 << 20),
    )(keys, values, segment.reshape(64, 128))
    tables = (span_order, counts)
    own = exchange(kv_packed)
    q_packed = pl.pallas_call(
        pack_q_kernel,
        out_shape=bf16(16, 2 * QR + 16, D),
        in_specs=[IN_VMEM] * 3 + [ANYWHERE],
        compiler_params=pltpu.CompilerParams(vmem_limit_bytes=16 << 20),
    )(queries, attn_out, out_grad, own)
    qpay = exchange(q_packed)

    near_1 = swap(own, 1)
    near_3 = swap(own, 3)
    far_a = swap(near_3[:8], 1)
    far_b = swap(near_1[8:], 3)
    own_pieces = (own, flip(own))
    near_pieces = (near_1, flip(near_1), near_3, flip(near_3))
    far_pieces = (far_a, far_b, flip(far_a), flip(far_b))

    def keys_scratch(spans):
        return pltpu.VMEM((spans, 2, 2, R, 2 * D), BF16)

    def sums_scratch(spans):
        return pltpu.VMEM((spans, 2, 2, R, D), F32)

    queries_scratch = pltpu.VMEM((NC, C, D), BF16)
    turned_scratch = pltpu.VMEM((NC + 1, 2 * D, C), BF16)
    total_scratch = pltpu.VMEM((NC + 1, 8, C), F32)
    dma = pltpu.SemaphoreType.DMA

    top, total, turned, grads, grads_turned = on_group(
        stats_kernel,
        [f32(NC, 1, C), f32(NC, 8, C), bf16(NC, D, C), bf16(NC, C, D), bf16(NC, 2 * D, C)],
        24,
        2,
        [queries_scratch, pltpu.VMEM((16, 16, D), BF16), keys_scratch(24)]
        + [turned_scratch, total_scratch, dma, dma],
        tables,
        (),
        (qpay,) + own_pieces + near_pieces,
        1,
    )
    group = bf16(16, 2 * R, D)
    half = bf16(8, 2 * R, D)
    logsum, dq, far_give, give_1, give_3, sum_a, sum_b, sum_1, sum_3 = on_group(
        far_near_kernel,
        [f32(NC, 1, C), f32(NC, D, C)] + [group] * 3 + [half] * 2 + [group] * 2,
        24,
        2,
        [queries_scratch, keys_scratch(24), keys_scratch(24), pltpu.VMEM((12, D, KB), BF16)]
        + [turned_scratch, sums_scratch(24), sums_scratch(24)]
        + [pltpu.VMEM((NC, 1, C), F32), total_scratch, dma, dma],
        tables,
        (top, total, grads, grads_turned),
        (qpay, turned) + far_pieces + near_pieces,
        6,
    )
    far_sum_a, far_sum_b, after = on_vmem(
        far_sum_kernel, [half, half, f32(8, D)], sum_a, sum_b, flip(far_give)
    )
    from_1 = swap(far_sum_a, 1)
    from_3 = swap(far_sum_b, 3)
    dq, keep, give = on_group(
        own_kernel,
        [bf16(16, QR, D), group, group],
        8,
        1,
        [queries_scratch, keys_scratch(8), keys_scratch(8), pltpu.VMEM((4, D, KB), BF16)]
        + [turned_scratch, sums_scratch(8), sums_scratch(8), pltpu.VMEM((NC, D, C), F32), dma],
        tables,
        (logsum, dq, grads, grads_turned, after),
        (qpay, turned) + own_pieces,
        5,
    )
    to_1, to_3 = on_vmem(
        near_sum_kernel, [group] * 2, sum_1, flip(give_1), sum_3, flip(give_3), from_1, from_3
    )
    sums, query_grad = on_vmem(
        last_sum_kernel,
        [group, bf16(R, 8 * G * D)],
        keep,
        flip(give),
        swap(to_1, 1),
        swap(to_3, 3),
        exchange(dq),
    )
    key_grad, value_grad = on_vmem(unpack_kernel, [bf16(R, 8 * D)] * 2, exchange(sums))
    return query_grad, key_grad, value_grad


def solution(mesh):
    fine = Mesh(mesh.devices.reshape(4, 2, 2, 2, 4), AXES)
    rows = P(AXES, None)
    return jax.shard_map(
        body,
        mesh=fine,
        in_specs=(rows,) * 5 + (P(), P()),
        out_specs=(rows,) * 3,
        check_vma=False,
    )
```

time: 578 us -> 149 us (0.26)
  matrix products: 249 us -> 0 us
  waiting for transfers between devices: 182 us -> 15.2 us
  other arithmetic: 70 us -> 0 us
  Pallas kernels: 0 us -> 64.6 us
  blocking collectives: 11.4 us -> 48.4 us
  local copies, waits for them, and re-layouts: 19.2 us -> 3.74 us
  between operations: 14 us -> 0.83 us
  starting transfers between devices: 26.4 us -> 13.6 us
    dot_general x96 -> x0, matrix products: 249 us -> none  [the longest x16 59.3 us: score_block(): jnp.einsum('rgqd,ngd->gqrn', queries4, key3, preferred_element_type=jnp.f...]
    reduce_scatter x2 -> x0, waiting for transfers between devices: 145 us -> none  [the longest x1 73.6 us: reduce_keys(): lax.psum_scatter(sums[0], 'ctx', scatter_dimension=0, tiled=True)]
    pallas_call x0 -> x9, Pallas kernels: none -> 64.6 us  [the longest x3 60.1 us: on_group(): pl.pallas_call(kernel, out_shape=outs, in_specs=[IN_SMEM] * 2 + [IN_VMEM]...]
    reduce_sum x16 -> x0, other arithmetic: 51.9 us -> none  [stats_step(): jnp.sum(weights, axis=-1)]
    all_to_all x1 -> x3, blocking collectives: 11.4 us -> 48.4 us  [exchange(): lax.all_to_all(array, SPREAD, split_axis=0, concat_axis=0, tiled=True)]
    all_to_all x7 -> x1, waiting for transfers between devices: 36.4 us -> 0.76 us  [exchange(): lax.all_to_all(array, SPREAD, split_axis=0, concat_axis=0, tiled=True)]
    all_to_all x7 -> x1, starting transfers between devices: 26.2 us -> 3.83 us  [exchange(): lax.all_to_all(array, SPREAD, split_axis=0, concat_axis=0, tiled=True)]
    ppermute x0 -> x17, waiting for transfers between devices: none -> 14.5 us  [the longest x8 13.2 us: swap(): return lax.ppermute(array, 'y', [(i, i ^ distance) for i in range(4)])]
  transfers between devices with their start and end apart: 11 -> 18, of which waited for: 7 -> 6; matrix products, arithmetic and copies ran while one was open for 23% -> 0% of each run, Pallas kernels for 0% -> 21%
where the time goes in v1:
time: 149 us; the launch traced here: 146 us
  Pallas kernels  64.6 us (43%)
  blocking collectives  48.4 us (32%)
  waiting for transfers between devices  15.2 us (10%)
  starting transfers between devices  13.6 us (9%)
  local copies, waits for them, and re-layouts  3.74 us (3%)
    pallas_call x3, Pallas kernels, on_group(): pl.pallas_call(kernel, out_shape=outs, in_specs=[IN_SMEM] * 2 + [IN_VMEM]...  60.1 us
    all_to_all x3, blocking collectives, exchange(): lax.all_to_all(array, SPREAD, split_axis=0, concat_axis=0, tiled=True)  48.4 us
    ppermute x8, waiting for transfers between devices, swap(): return lax.ppermute(array, 'y', [(i, i ^ distance) for i in range(4)])  13.2 us
    ppermute x8, starting transfers between devices, swap(): return lax.ppermute(array, 'y', [(i, i ^ distance) for i in range(4)])  8.73 us
    all_to_all x1, starting transfers between devices, exchange(): lax.all_to_all(array, SPREAD, split_axis=0, concat_axis=0, tiled=True)  3.83 us
    unnamed x18, local copies, waits for them, and re-layouts  3.71 us
  transfers between devices with their start and end apart: 18, of which 6 were waited for; matrix products, arithmetic and copies ran while one was open for 0% of the time, Pallas kernels for 21%

profile of v1, /device:TPU:0, one launch (start us, length us, event | category | flops | bytes accessed | tf_op | source)
XLA Modules:
  0.0 146.4 jit_solution(3429554692734544780)
XLA Ops:
  0.7 1.0 copy-done.5
  1.6 0.9 copy-done.6
  2.5 0.8 copy-done.7
  3.3 0.7 shard_map.94
  4.0 19.3 %all_to_all.20.after.own = bf16[16,128,128]{2,1,0:T(8,128)(2,1)S(1)} all-to-all(bf16[16,128,128]{2,1,0:T(8,128)(2,1)S(1)} %get-tuple-element.32), channel_id=1, replica_groups=mesh['z'=4,'core'=2,'xh'=2,'xl'=2,'y'=4] {'xh','xl','z'}, dimensions={0} | all-to-all | bytes 1048576 | tf_op jit(solution)/shard_map/all_to_all | solution.py:639
  23.3 3.0 %collective-permute-start.3 = (bf16[16,128,128]{2,1,0:T(8,128)(2,1)S(1)}, bf16[16,128,128]{2,1,0:T(8,128)(2,1)S(1)}, u32[]{:S(2)}, u32[]{:S(2)}) collective-permute-start(bf16[16,128,128]{2,1,0:T(8,128)(2,1)S(1)} %all_to_all.20.after.own), channel_id=1, source_target_pairs={{0,3},{1,2},{2,1},{3,0},{4,7},{5,6},{6,5},{7,4},{8,11},{9,10},{10,... | collective-permute-start | bytes 1572872 | tf_op jit(solution)/shard_map/ppermute | solution.py:647
  26.3 0.1 collective-permute-start.1
  26.4 1.0 copy-done.4
  27.5 1.7 %shard_map.95 = bf16[16,272,128]{2,1,0:T(8,128)(2,1)} custom-call(bf16[64,4096]{1,0:T(8,128)(2,1)S(1)} %copy-done.2, bf16[64,4096]{1,0:T(8,128)(2,1)S(1)} %copy-done.3, bf16[64,4096]{1,0:T(8,128)(2,1)S(1)} %copy-done.4, bf16[16,128,128]{2,1,0:T(8,128)(2,1)S(1)} %all_to_all.20.after.own), custom_call_target="tpu_custom_call" | custom-call | tf_op jit(solution)/shard_map/pallas_call | solution.py:659
  29.2 3.8 %all-to-all-start.1 = ((bf16[16,272,128]{2,1,0:T(8,128)(2,1)}), bf16[16,272,128]{2,1,0:T(8,128)(2,1)S(1)}, u32[]{:S(2)}, u32[]{:S(2)}) async-start(bf16[16,272,128]{2,1,0:T(8,128)(2,1)} %shard_map.95), calls=%async_computation.1 | async-start | bytes 2228224 | tf_op jit(solution)/shard_map/all_to_all | solution.py:639
  33.0 0.1 collective-permute-start
  33.1 3.7 %collective-permute-done.3.near_3 = bf16[16,128,128]{2,1,0:T(8,128)(2,1)S(1)} collective-permute-done((bf16[16,128,128]{2,1,0:T(8,128)(2,1)S(1)}, bf16[16,128,128]{2,1,0:T(8,128)(2,1)S(1)}, u32[]{:S(2)}, u32[]{:S(2)}) %collective-permute-start.3) | collective-permute-done | bytes 524320 | tf_op jit(solution)/shard_map/ppermute | solution.py:647
  36.8 0.0 collective-permute-start.4
  36.8 1.5 collective-permute-done.1.near_1
  38.2 0.0 collective-permute-start.2
  38.2 0.4 collective-permute-start.5
  38.6 1.8 %collective-permute-start.6 = (bf16[8,128,128]{2,1,0:T(8,128)(2,1)S(1)}, bf16[8,128,128]{2,1,0:T(8,128)(2,1)}, u32[]{:S(2)}, u32[]{:S(2)}) collective-permute-start(bf16[8,128,128]{2,1,0:T(8,128)(2,1)S(1)} %slice.9), channel_id=1, source_target_pairs={{0,3},{1,2},{2,1},{3,0},{4,7},{5,6},{6,5},{7,4},{8,11},{9,10},{10,... | collective-permute-start | bytes 786440 | tf_op jit(solution)/shard_map/ppermute | solution.py:647
  40.4 6.6 %collective-permute-done.5.far_a = bf16[8,128,128]{2,1,0:T(8,128)(2,1)S(1)} collective-permute-done((bf16[8,128,128]{2,1,0:T(8,128)(2,1)S(1)}, bf16[8,128,128]{2,1,0:T(8,128)(2,1)S(1)}, u32[]{:S(2)}, u32[]{:S(2)}) %collective-permute-start.5) | collective-permute-done | bytes 262176 | tf_op jit(solution)/shard_map/ppermute | solution.py:647
  47.0 0.0 collective-permute-start.7
  47.0 1.4 collective-permute-done.6.far_b
  48.5 0.0 collective-permute-start.8
  48.5 0.0 collective-permute-done.own_o
  48.5 0.8 all-to-all-done.1.qpay
  49.3 16.0 %shard_map.96 = (f32[8,1,256]{2,1,0:T(1,128)S(1)}, f32[8,8,256]{2,1,0:T(8,128)S(1)}, bf16[8,128,256]{2,1,0:T(8,128)(2,1)S(1)}, bf16[8,256,128]{2,1,0:T(8,128)(2,1)S(1)}, bf16[8,256,256]{2,1,0:T(8,128)(2,1)S(1)}) custom-call(s32[32]{0:T(128)S(1)} %copy-done.8, s32[2]{0:T(128)S(1)} %get-tuple-element.31.counts, bf16[16,272,128]{2,1,0:T(8,128)(2,1)S(1)} %all-to-all-done.1.qpay, ...), custom_call_target="tpu_custom_call" | custom-call | flops 1073741824 | bytes 4194304 | tf_op jit(solution)/shard_map/pallas_call | solution.py:626
  65.3 0.0 collective-permute-done.8.far_bo
  65.3 30.9 %shard_map.97 = (f32[8,1,256]{2,1,0:T(1,128)S(1)}, f32[8,128,256]{2,1,0:T(8,128)S(1)}, bf16[16,128,128]{2,1,0:T(8,128)(2,1)S(1)}, bf16[16,128,128]{2,1,0:T(8,128...) custom-call(s32[32]{0:T(128)S(1)} %copy-done.8, ...), custom_call_target="tpu_custom_call" | custom-call | flops 6442450944 | bytes 4194304 | tf_op jit(solution)/shard_map/pallas_call | solution.py:626
  96.2 0.1 collective-permute-start.9
  96.2 0.5 collective-permute-start.11
  96.7 0.1 collective-permute-start.12
  96.8 1.3 collective-permute-done.9.got
  98.1 0.1 shard_map.98
  98.3 0.1 collective-permute-start.13
  98.4 0.1 collective-permute-start.14
  98.5 13.2 %shard_map.99 = (bf16[16,128,128]{2,1,0:T(8,128)(2,1)S(1)}, bf16[16,128,128]{2,1,0:T(8,128)(2,1)S(1)}, bf16[16,128,128]{2,1,0:T(8,128)(2,1)S(1)}) custom-call(s32[32]{0:T(128)S(1)} %copy-done.8, s32[2]{0:T(128)S(1)} %get-tuple-element.31.counts, f32[8,1,256]{2,1,0:T(1,128)S(1)} %get-tuple-element.38.logsum, f32[8,128,256]{2,1,0:T(8,128)S(1)} %get-tuple-element.39.dq_in, ...), custom_call_target="tpu_custom_call" | custom-call | flops 1789569664 | bytes 4194304 | tf_op jit(solution)/shard_map/pallas_call | solution.py:626
  111.7 0.2 collective-permute-start.10
  112.0 0.0 collective-permute-done.11.got_1
  112.0 0.0 collective-permute-done.12.got_3
  112.0 0.0 collective-permute-done.13.from_1
  112.0 0.3 shard_map.100
  112.3 0.9 collective-permute-start.15
  113.2 2.3 %collective-permute-start.16 = (bf16[16,128,128]{2,1,0:T(8,128)(2,1)S(1)}, bf16[16,128,128]{2,1,0:T(8,128)(2,1)S(1)}, u32[]{:S(2)}, u32[]{:S(2)}) collective-permute-start(bf16[16,128,128]{2,1,0:T(8,128)(2,1)S(1)} %get-tuple-element.53), channel_id=1, source_target_pairs={{0,3},{1,2},{2,1},{3,0},{4,7},{5,6},{6,5},{7,4},{8,11},{9,10},{10,... | collective-permute-start | bytes 1572872 | tf_op jit(solution)/shard_map/ppermute | solution.py:647
  115.5 15.2 %all_to_all.21.dq = bf16[16,128,128]{2,1,0:T(8,128)(2,1)S(1)} all-to-all(bf16[16,128,128]{2,1,0:T(8,128)(2,1)S(1)} %get-tuple-element.54), channel_id=1, replica_groups=mesh['z'=4,'core'=2,'xh'=2,'xl'=2,'y'=4] {'xh','xl','z'}, dimensions={0} | all-to-all | bytes 1048576 | tf_op jit(solution)/shard_map/all_to_all | solution.py:639
  130.7 0.0 collective-permute-done.10.got
  130.7 0.0 collective-permute-done.15.near_1
  130.7 0.0 collective-permute-done.16.near_3
  130.7 0.9 shard_map.101
  131.7 13.9 %all_to_all.22.got = bf16[16,128,128]{2,1,0:T(8,128)(2,1)S(1)} all-to-all(bf16[16,128,128]{2,1,0:T(8,128)(2,1)S(1)} %get-tuple-element.56), channel_id=1, replica_groups=mesh['z'=4,'core'=2,'xh'=2,'xl'=2,'y'=4] {'xh','xl','z'}, dimensions={0} | all-to-all | bytes 1048576 | tf_op jit(solution)/shard_map/all_to_all | solution.py:639
  145.6 0.8 shard_map.102
  (20 shorter events, 0.1 us)
Async XLA Ops:
  0.6 25.8 %copy-start.3 = (bf16[64,4096]{1,0:T(8,128)(2,1)S(1)}, bf16[64,4096]{1,0:T(8,128)(2,1)}, u32[]{:S(2)}) copy-start(bf16[64,4096]{1,0:T(8,128)(2,1)} %saved.1) | copy-start | bytes 1572868
  0.6 25.8 %copy-start.2 = (bf16[64,4096]{1,0:T(8,128)(2,1)S(1)}, bf16[64,4096]{1,0:T(8,128)(2,1)}, u32[]{:S(2)}) copy-start(bf16[64,4096]{1,0:T(8,128)(2,1)} %queries.1) | copy-start | bytes 1572868
  0.7 1.0 copy-start.5
  1.6 0.9 copy-start.6
  2.5 0.8 copy-start.7
  23.3 13.5 %collective-permute-start.3 = (bf16[16,128,128]{2,1,0:T(8,128)(2,1)S(1)}, bf16[16,128,128]{2,1,0:T(8,128)(2,1)S(1)}, u32[]{:S(2)}, u32[]{:S(2)}) collective-permute-start(bf16[16,128,128]{2,1,0:T(8,128)(2,1)S(1)} %all_to_all.20.after.own), channel_id=1, source_target_pairs={{0,3},{1,2},{2,1},{3,0},{4,7},{5,6},{6,5},{7,4},{8,11},{9,10},{10,... | collective-permute-start | bytes 1572872 | tf_op jit(solution)/shard_map/ppermute | solution.py:647
  26.3 11.9 %collective-permute-start.1 = (bf16[16,128,128]{2,1,0:T(8,128)(2,1)S(1)}, bf16[16,128,128]{2,1,0:T(8,128)(2,1)S(1)}, u32[]{:S(2)}, u32[]{:S(2)}) collective-permute-start(bf16[16,128,128]{2,1,0:T(8,128)(2,1)S(1)} %all_to_all.20.after.own), channel_id=1, source_target_pairs={{0,1},{1,0},{2,3},{3,2},{4,5},{5,4},{6,7},{7,6},{8,9},{9,8},{10,11... | collective-permute-start | bytes 1572872 | tf_op jit(solution)/shard_map/ppermute | solution.py:647
  26.4 1.0 copy-start.4
  29.2 20.1 %copy-start.8 = (s32[32]{0:T(128)S(1)}, s32[32]{0:T(128)}, u32[]{:S(2)}) copy-start(s32[32]{0:T(128)} %order.5) | copy-start | bytes 388
  29.2 20.1 %all-to-all-start.1 = ((bf16[16,272,128]{2,1,0:T(8,128)(2,1)}), bf16[16,272,128]{2,1,0:T(8,128)(2,1)S(1)}, u32[]{:S(2)}, u32[]{:S(2)}) async-start(bf16[16,272,128]{2,1,0:T(8,128)(2,1)} %shard_map.95), calls=%async_computation.1 | async-start | bytes 2228224 | tf_op jit(solution)/shard_map/all_to_all | solution.py:639
  33.0 15.5 %collective-permute-start = (bf16[16,128,128]{2,1,0:T(8,128)(2,1)S(1)}, bf16[16,128,128]{2,1,0:T(8,128)(2,1)S(1)}, u32[]{:S(2)}, u32[]{:S(2)}) collective-permute-start(bf16[16,128,128]{2,1,0:T(8,128)(2,1)S(1)} %all_to_all.20.after.own), channel_id=1, source_target_pairs={{0,16},{16,0},{1,17},{17,1},{2,18},{18,2},{3,19},{19,3},{4,20},{20... | collective-permute-start | bytes 1572872 | tf_op jit(solution)/shard_map/ppermute | solution.py:643
  36.8 12.5 %collective-permute-start.4 = (bf16[16,128,128]{2,1,0:T(8,128)(2,1)S(1)}, bf16[16,128,128]{2,1,0:T(8,128)(2,1)}, u32[]{:S(2)}, u32[]{:S(2)}) collective-permute-start(bf16[16,128,128]{2,1,0:T(8,128)(2,1)S(1)} %collective-permute-done.3.near_3), channel_id=1, source_target_pairs={{0,16},{16,0},{1,17},{17,1},{2,18},{18,2},{3,19},{19,3},{4,20},{20... | collective-permute-start | bytes 1572872 | tf_op jit(solution)/shard_map/ppermute | solution.py:643
  38.2 11.0 %collective-permute-start.2 = (bf16[16,128,128]{2,1,0:T(8,128)(2,1)S(1)}, bf16[16,128,128]{2,1,0:T(8,128)(2,1)}, u32[]{:S(2)}, u32[]{:S(2)}) collective-permute-start(bf16[16,128,128]{2,1,0:T(8,128)(2,1)S(1)} %collective-permute-done.1.near_1), channel_id=1, source_target_pairs={{0,16},{16,0},{1,17},{17,1},{2,18},{18,2},{3,19},{19,3},{4,20},{20... | collective-permute-start | bytes 1572872 | tf_op jit(solution)/shard_map/ppermute | solution.py:643
  38.2 8.8 %collective-permute-start.5 = (bf16[8,128,128]{2,1,0:T(8,128)(2,1)S(1)}, bf16[8,128,128]{2,1,0:T(8,128)(2,1)S(1)}, u32[]{:S(2)}, u32[]{:S(2)}) collective-permute-start(bf16[8,128,128]{2,1,0:T(8,128)(2,1)S(1)} %slice.8), channel_id=1, source_target_pairs={{0,1},{1,0},{2,3},{3,2},{4,5},{5,4},{6,7},{7,6},{8,9},{9,8},{10,11... | collective-permute-start | bytes 786440 | tf_op jit(solution)/shard_map/ppermute | solution.py:647
  38.6 9.8 %collective-permute-start.6 = (bf16[8,128,128]{2,1,0:T(8,128)(2,1)S(1)}, bf16[8,128,128]{2,1,0:T(8,128)(2,1)}, u32[]{:S(2)}, u32[]{:S(2)}) collective-permute-start(bf16[8,128,128]{2,1,0:T(8,128)(2,1)S(1)} %slice.9), channel_id=1, source_target_pairs={{0,3},{1,2},{2,1},{3,0},{4,7},{5,6},{6,5},{7,4},{8,11},{9,10},{10,... | collective-permute-start | bytes 786440 | tf_op jit(solution)/shard_map/ppermute | solution.py:647
  47.0 18.2 %collective-permute-start.7 = (bf16[8,128,128]{2,1,0:T(8,128)(2,1)S(1)}, bf16[8,128,128]{2,1,0:T(8,128)(2,1)}, u32[]{:S(2)}, u32[]{:S(2)}) collective-permute-start(bf16[8,128,128]{2,1,0:T(8,128)(2,1)S(1)} %collective-permute-done.5.far_a), channel_id=1, source_target_pairs={{0,16},{16,0},{1,17},{17,1},{2,18},{18,2},{3,19},{19,3},{4,20},{20... | collective-permute-start | bytes 786440 | tf_op jit(solution)/shard_map/ppermute | solution.py:643
  48.5 16.8 %collective-permute-start.8 = (bf16[8,128,128]{2,1,0:T(8,128)(2,1)}, bf16[8,128,128]{2,1,0:T(8,128)(2,1)}, u32[]{:S(2)}, u32[]{:S(2)}) collective-permute-start(bf16[8,128,128]{2,1,0:T(8,128)(2,1)} %collective-permute-done.6.far_b), channel_id=1, source_target_pairs={{0,16},{16,0},{1,17},{17,1},{2,18},{18,2},{3,19},{19,3},{4,20},{20... | collective-permute-start | bytes 786440 | tf_op jit(solution)/shard_map/ppermute | solution.py:643
  49.2 16.0 %copy-start = (bf16[16,272,128]{2,1,0:T(8,128)(2,1)}, bf16[16,272,128]{2,1,0:T(8,128)(2,1)S(1)}, u32[]{:S(2)}) copy-start(bf16[16,272,128]{2,1,0:T(8,128)(2,1)S(1)} %all-to-all-done.1.qpay) | copy-start | bytes 3342340
  65.3 33.2 %copy-start.1 = (bf16[16,272,128]{2,1,0:T(8,128)(2,1)S(1)}, bf16[16,272,128]{2,1,0:T(8,128)(2,1)}, u32[]{:S(2)}) copy-start(bf16[16,272,128]{2,1,0:T(8,128)(2,1)} %copy-done) | copy-start | bytes 3342340
  96.2 2.0 %collective-permute-start.9 = (bf16[16,128,128]{2,1,0:T(8,128)(2,1)S(1)}, bf16[16,128,128]{2,1,0:T(8,128)(2,1)S(1)}, u32[]{:S(2)}, u32[]{:S(2)}) collective-permute-start(bf16[16,128,128]{2,1,0:T(8,128)(2,1)S(1)} %get-tuple-element.42), channel_id=1, source_target_pairs={{0,16},{16,0},{1,17},{17,1},{2,18},{18,2},{3,19},{19,3},{4,20},{20... | collective-permute-start | bytes 1572872 | tf_op jit(solution)/shard_map/ppermute | solution.py:643
  96.2 15.7 %collective-permute-start.11 = (bf16[16,128,128]{2,1,0:T(8,128)(2,1)S(1)}, bf16[16,128,128]{2,1,0:T(8,128)(2,1)S(1)}, u32[]{:S(2)}, u32[]{:S(2)}) collective-permute-start(bf16[16,128,128]{2,1,0:T(8,128)(2,1)S(1)} %get-tuple-element.47), channel_id=1, source_target_pairs={{0,16},{16,0},{1,17},{17,1},{2,18},{18,2},{3,19},{19,3},{4,20},{20... | collective-permute-start | bytes 1572872 | tf_op jit(solution)/shard_map/ppermute | solution.py:643
  96.7 15.2 %collective-permute-start.12 = (bf16[16,128,128]{2,1,0:T(8,128)(2,1)S(1)}, bf16[16,128,128]{2,1,0:T(8,128)(2,1)S(1)}, u32[]{:S(2)}, u32[]{:S(2)}) collective-permute-start(bf16[16,128,128]{2,1,0:T(8,128)(2,1)S(1)} %get-tuple-element.49), channel_id=1, source_target_pairs={{0,16},{16,0},{1,17},{17,1},{2,18},{18,2},{3,19},{19,3},{4,20},{20... | collective-permute-start | bytes 1572872 | tf_op jit(solution)/shard_map/ppermute | solution.py:643
  98.3 13.7 %collective-permute-start.13 = (bf16[8,128,128]{2,1,0:T(8,128)(2,1)S(1)}, bf16[8,128,128]{2,1,0:T(8,128)(2,1)S(1)}, u32[]{:S(2)}, u32[]{:S(2)}) collective-permute-start(bf16[8,128,128]{2,1,0:T(8,128)(2,1)S(1)} %get-tuple-element.50), channel_id=1, source_target_pairs={{0,1},{1,0},{2,3},{3,2},{4,5},{5,4},{6,7},{7,6},{8,9},{9,8},{10,11... | collective-permute-start | bytes 786440 | tf_op jit(solution)/shard_map/ppermute | solution.py:647
  98.4 13.6 %collective-permute-start.14 = (bf16[8,128,128]{2,1,0:T(8,128)(2,1)S(1)}, bf16[8,128,128]{2,1,0:T(8,128)(2,1)S(1)}, u32[]{:S(2)}, u32[]{:S(2)}) collective-permute-start(bf16[8,128,128]{2,1,0:T(8,128)(2,1)S(1)} %get-tuple-element.51), channel_id=1, source_target_pairs={{0,3},{1,2},{2,1},{3,0},{4,7},{5,6},{6,5},{7,4},{8,11},{9,10},{10,... | collective-permute-start | bytes 786440 | tf_op jit(solution)/shard_map/ppermute | solution.py:647
  111.7 19.0 %collective-permute-start.10 = (bf16[16,128,128]{2,1,0:T(8,128)(2,1)S(1)}, bf16[16,128,128]{2,1,0:T(8,128)(2,1)S(1)}, u32[]{:S(2)}, u32[]{:S(2)}) collective-permute-start(bf16[16,128,128]{2,1,0:T(8,128)(2,1)S(1)} %get-tuple-element.45), channel_id=1, source_target_pairs={{0,16},{16,0},{1,17},{17,1},{2,18},{18,2},{3,19},{19,3},{4,20},{20... | collective-permute-start | bytes 1572872 | tf_op jit(solution)/shard_map/ppermute | solution.py:643
  112.3 18.4 %collective-permute-start.15 = (bf16[16,128,128]{2,1,0:T(8,128)(2,1)S(1)}, bf16[16,128,128]{2,1,0:T(8,128)(2,1)S(1)}, u32[]{:S(2)}, u32[]{:S(2)}) collective-permute-start(bf16[16,128,128]{2,1,0:T(8,128)(2,1)S(1)} %get-tuple-element.52), channel_id=1, source_target_pairs={{0,1},{1,0},{2,3},{3,2},{4,5},{5,4},{6,7},{7,6},{8,9},{9,8},{10,11... | collective-permute-start | bytes 1572872 | tf_op jit(solution)/shard_map/ppermute | solution.py:647
  113.2 17.5 %collective-permute-start.16 = (bf16[16,128,128]{2,1,0:T(8,128)(2,1)S(1)}, bf16[16,128,128]{2,1,0:T(8,128)(2,1)S(1)}, u32[]{:S(2)}, u32[]{:S(2)}) collective-permute-start(bf16[16,128,128]{2,1,0:T(8,128)(2,1)S(1)} %get-tuple-element.53), channel_id=1, source_target_pairs={{0,3},{1,2},{2,1},{3,0},{4,7},{5,6},{6,5},{7,4},{8,11},{9,10},{10,... | collective-permute-start | bytes 1572872 | tf_op jit(solution)/shard_map/ppermute | solution.py:647
